TPU v7x, 32 devices: a whole 2x2x4 slice. The times are simulated.
32 devices in a mesh: wide: 8 (over z, x), narrow: 4 (over y, core).
Axes of the slice: x: 2, y: 2, z: 4, core: 2. Of those that a mesh axis runs over, the one named last changes fastest.
Arguments:
- target_ids: int32 [32, 192], P(('wide', 'narrow')), may hold values from 0 to 250111, as said below
- target_lengths: int32 [32], P(('wide', 'narrow')), may hold values from 1 to 192, 4608 in all
- bucket_table: int32 [192], replicated, may hold values from 0 to 31, as said below
- memory: bfloat16 [32, 1536, 768], P(('wide', 'narrow')), may hold values from -6 to 6
- table: bfloat16 [250112, 768], P(('wide', 'narrow')), may hold values from -6 to 6
- self_qkv: bfloat16 [1769472], P(('wide', 'narrow')), may hold values from -0.21875 to 0.21875
- self_out: bfloat16 [589824], P(('wide', 'narrow')), may hold values from -1.75 to 1.75
- cross_q: bfloat16 [589824], P(('wide', 'narrow')), may hold values from -0.21875 to 0.21875
- cross_kv: bfloat16 [1179648], P(('wide', 'narrow')), may hold values from -0.21875 to 0.21875
- cross_out: bfloat16 [589824], P(('wide', 'narrow')), may hold values from -3.5 to 3.5
- ffn_in: bfloat16 [3145728], P(('wide', 'narrow')), may hold values from -0.21875 to 0.21875
- ffn_out: bfloat16 [1572864], P(('wide', 'narrow')), may hold values from -0.125 to 0.125
- gains: float32 [3, 768], replicated, may hold values from 0.5 to 1.5
- relative_bias: float32 [32, 12], replicated, may hold values from -4 to 4
- cotangent: float32 [32, 192, 768], P(('wide', 'narrow')), may hold values from -6 to 6
Outputs:
- hidden: float32 [32, 192, 768], P(('wide', 'narrow'))
- memory_grad: bfloat16 [32, 1536, 768], P(('wide', 'narrow'))
- table_grad: float32 [250112, 768], P(('wide', 'narrow'))
- self_qkv_grad: float32 [1769472], P(('wide', 'narrow'))
- self_out_grad: float32 [589824], P(('wide', 'narrow'))
- cross_q_grad: float32 [589824], P(('wide', 'narrow'))
- cross_kv_grad: float32 [1179648], P(('wide', 'narrow'))
- cross_out_grad: float32 [589824], P(('wide', 'narrow'))
- ffn_in_grad: float32 [3145728], P(('wide', 'narrow'))
- ffn_out_grad: float32 [1572864], P(('wide', 'narrow'))
- gains_grad: float32 [3, 768], replicated
- bias_grad: float32 [32, 12], replicated
Inputs may be any that keep to these rules, and one draw needn't show every extreme that they name: `target_ids`: of the 192 ids of one device's 1 pairs, at most 12 lie in any one block of 7816 table rows (rows c * 7816 to (c + 1) * 7816 - 1); in every draw one such block holds exactly 12 of every device's ids. `target_lengths`: positions at or beyond a pair's length are padding; the lengths of all pairs sum to 4608 and some pair has length 192. `bucket_table`: nondecreasing in the distance, 0 at distance 0 and 31 at distance 192 - 1.
All inputs are finite; a program needn't handle non-finite values. No bound on the sum of `target_lengths` on one device may be relied on, other than what follows from the above.
Results may differ from a plain program's by a relative error of at most 0.02.
Values may be sent and summed in bfloat16 or wider, within the bound.
A program may use at most 256 MiB of HBM per device.

v0:
```python
import jax
import jax.numpy as jnp
from jax import lax
from jax.sharding import PartitionSpec as P

epsilon = 1e-06
blocked = -1e30
top_precision = lax.Precision.HIGHEST


def rms_scaled(inputs, gain):
    return inputs * lax.rsqrt(jnp.mean(inputs * inputs, axis=-1, keepdims=True) + epsilon) * gain


def norm_backward(inputs, gain, upstream):
    unused, pullback = jax.vjp(rms_scaled, inputs, gain)
    return pullback(upstream)


def gated(gate, upper):
    return jax.nn.gelu(gate, approximate=True) * upper


def matmul(left, right):
    return jnp.dot(left, right, preferred_element_type=jnp.float32)


def outer_sum(left, right):
    return lax.dot_general(
        left, right, (((0,), (0,)), ((), ())), preferred_element_type=jnp.float32
    )


def back_product(left, right):
    return lax.dot_general(
        left, right, (((1,), (1,)), ((), ())), preferred_element_type=jnp.float32
    )


def softmax_stats(scores):
    row_peak = jnp.max(scores, axis=-1, keepdims=True)
    exponent = jnp.exp(scores - row_peak)
    row_total = jnp.sum(exponent, axis=-1, keepdims=True)
    return (exponent / row_total, row_peak + jnp.log(row_total))


def score_self(queries, keys_self, expanded_bias, allowed, score_scale):
    scores = jnp.einsum("pqhd,pkhd->phqk", queries, keys_self, preferred_element_type=jnp.float32)
    scores = scores * score_scale + expanded_bias[None]
    return jnp.where(allowed[:, None], scores, blocked)


def unpack(flats, model_width, ffn_width):
    return (
        flats[0].reshape(model_width, 3 * model_width),
        flats[1].reshape(model_width, model_width),
        flats[2].reshape(model_width, model_width),
        flats[3].reshape(model_width, 2 * model_width),
        flats[4].reshape(model_width, model_width),
        flats[5].reshape(model_width, 2 * ffn_width),
        flats[6].reshape(ffn_width, model_width),
    )


def body(
    target_ids,
    target_lengths,
    bucket_table,
    memory,
    table,
    self_qkv,
    self_out,
    cross_q,
    cross_kv,
    cross_out,
    ffn_in,
    ffn_out,
    gains,
    relative_bias,
    cotangent,
):
    pair_count, seq_len = target_ids.shape
    model_width = table.shape[1]
    head_count = relative_bias.shape[1]
    head_size = model_width // head_count
    bucket_count = relative_bias.shape[0]
    memory_len = memory.shape[1]
    wide_count = lax.axis_size("wide")
    narrow_count = lax.axis_size("narrow")
    owner_count = wide_count * narrow_count
    ffn_width = ffn_out.shape[0] * owner_count // model_width
    token_count = pair_count * seq_len
    shard_rows = table.shape[0]
    capacity = max(2, (2 * token_count + owner_count - 1) // owner_count)
    score_scale = head_size ** (-0.5)
    positions = jnp.arange(seq_len, dtype=jnp.int32)
    valid_rows = (positions[None, :] < target_lengths[:, None]).astype(jnp.float32)
    valid_flat = valid_rows.reshape(token_count, 1)
    allowed = (positions[None, :] <= positions[:, None])[None] & (valid_rows[:, None, :] > 0.0)
    distance = jnp.clip(positions[:, None] - positions[None, :], 0, seq_len - 1)
    bucket_ids = jnp.take(bucket_table, distance)
    bucket_indicator = (
        bucket_ids[None, :, :] == jnp.arange(bucket_count, dtype=jnp.int32)[:, None, None]
    ).astype(jnp.float32)
    expanded_bias = jnp.einsum(
        "awj,ar->rwj", bucket_indicator, relative_bias, precision=top_precision
    )
    flat_ids = target_ids.reshape(token_count)
    owner_index = flat_ids // shard_rows
    owner_hits = (owner_index[:, None] == jnp.arange(owner_count, dtype=jnp.int32)[None, :]).astype(
        jnp.int32
    )
    rank_within = jnp.sum(jnp.cumsum(owner_hits, axis=0) * owner_hits, axis=1) - 1
    slot_index = owner_index * capacity + rank_within
    outgoing = (
        jnp.full((owner_count * capacity,), -1, jnp.int32)
        .at[slot_index]
        .set(flat_ids - owner_index * shard_rows)
    )
    requests = lax.all_to_all(
        lax.all_to_all(
            outgoing.reshape(wide_count, narrow_count, capacity),
            "wide",
            split_axis=0,
            concat_axis=0,
            tiled=True,
        ),
        "narrow",
        split_axis=1,
        concat_axis=1,
        tiled=True,
    )
    found = jnp.where(
        (requests >= 0)[:, :, :, None], table[jnp.maximum(requests, 0)], jnp.zeros((), jnp.bfloat16)
    )
    arrived = lax.all_to_all(
        lax.all_to_all(found, "wide", split_axis=0, concat_axis=0, tiled=True),
        "narrow",
        split_axis=1,
        concat_axis=1,
        tiled=True,
    )
    embedded = (
        arrived.reshape(owner_count * capacity, model_width)[slot_index].astype(jnp.float32)
        * valid_flat
    )
    shards = (self_qkv, self_out, cross_q, cross_kv, cross_out, ffn_in, ffn_out)
    gathered = (
        lax.all_gather(shards[0], ("wide", "narrow"), axis=0, tiled=True),
        lax.all_gather(shards[1], ("wide", "narrow"), axis=0, tiled=True),
        lax.all_gather(shards[2], ("wide", "narrow"), axis=0, tiled=True),
        lax.all_gather(shards[3], ("wide", "narrow"), axis=0, tiled=True),
        lax.all_gather(shards[4], ("wide", "narrow"), axis=0, tiled=True),
        lax.all_gather(shards[5], ("wide", "narrow"), axis=0, tiled=True),
        lax.all_gather(shards[6], ("wide", "narrow"), axis=0, tiled=True),
    )
    w_qkv, w_out1, w_q2, w_kv2, second_output_weight, w_in, w_out3 = unpack(
        gathered, model_width, ffn_width
    )
    self_normalized = rms_scaled(embedded, gains[0]).astype(jnp.bfloat16)
    merged_heads = (
        matmul(self_normalized, w_qkv)
        .astype(jnp.bfloat16)
        .reshape(pair_count, seq_len, 3, head_count, head_size)
    )
    queries = merged_heads[:, :, 0]
    keys_self = merged_heads[:, :, 1]
    values_self = merged_heads[:, :, 2]
    self_probs, self_lse = softmax_stats(
        score_self(queries, keys_self, expanded_bias, allowed, score_scale)
    )
    self_mixed = (
        jnp.einsum(
            "phqk,pkhd->pqhd",
            self_probs.astype(jnp.bfloat16),
            values_self,
            preferred_element_type=jnp.float32,
        )
        .astype(jnp.bfloat16)
        .reshape(token_count, model_width)
    )
    after_self = embedded + matmul(self_mixed, w_out1)
    normed_cross = rms_scaled(after_self, gains[1]).astype(jnp.bfloat16)
    cross_queries = (
        matmul(normed_cross, w_q2)
        .astype(jnp.bfloat16)
        .reshape(pair_count, seq_len, head_count, head_size)
    )

    def cross_forward(pair_items):
        query_rows, memory_rows = pair_items
        key_values = matmul(memory_rows, w_kv2).astype(jnp.bfloat16)
        keys_pair = key_values[:, :model_width].reshape(memory_len, head_count, head_size)
        values_pair = key_values[:, model_width:].reshape(memory_len, head_count, head_size)
        scores = (
            jnp.einsum("qhd,khd->hqk", query_rows, keys_pair, preferred_element_type=jnp.float32)
            * score_scale
        )
        probs, lse_rows = softmax_stats(scores)
        blended = jnp.einsum(
            "hqk,khd->qhd",
            probs.astype(jnp.bfloat16),
            values_pair,
            preferred_element_type=jnp.float32,
        )
        return (blended.astype(jnp.bfloat16).reshape(seq_len, model_width), lse_rows, key_values)

    cross_mixed, cross_lse, kept_kv = lax.map(cross_forward, (cross_queries, memory))
    cross_flat = cross_mixed.reshape(token_count, model_width)
    after_cross = after_self + matmul(cross_flat, second_output_weight)
    normed_ffn = rms_scaled(after_cross, gains[2]).astype(jnp.bfloat16)
    gate_up = matmul(normed_ffn, w_in)
    activated = gated(gate_up[:, :ffn_width], gate_up[:, ffn_width:]).astype(jnp.bfloat16)
    final_state = after_cross + matmul(activated, w_out3)
    hidden = final_state.reshape(pair_count, seq_len, model_width) * valid_rows[:, :, None]
    gathered = (
        lax.all_gather(shards[0], ("wide", "narrow"), axis=0, tiled=True),
        lax.all_gather(shards[1], ("wide", "narrow"), axis=0, tiled=True),
        lax.all_gather(shards[2], ("wide", "narrow"), axis=0, tiled=True),
        lax.all_gather(shards[3], ("wide", "narrow"), axis=0, tiled=True),
        lax.all_gather(shards[4], ("wide", "narrow"), axis=0, tiled=True),
        lax.all_gather(shards[5], ("wide", "narrow"), axis=0, tiled=True),
        lax.all_gather(shards[6], ("wide", "narrow"), axis=0, tiled=True),
    )
    w_qkv, w_out1, w_q2, w_kv2, second_output_weight, w_in, w_out3 = unpack(
        gathered, model_width, ffn_width
    )
    upstream = (cotangent * valid_rows[:, :, None]).reshape(token_count, model_width)
    grad_branch3 = upstream.astype(jnp.bfloat16)
    grad_w_out3 = outer_sum(activated, grad_branch3)
    grad_act = back_product(grad_branch3, w_out3)
    unused, gate_pull = jax.vjp(gated, gate_up[:, :ffn_width], gate_up[:, ffn_width:])
    grad_gate, grad_upper = gate_pull(grad_act)
    grad_gate_up = jnp.concatenate([grad_gate, grad_upper], axis=1).astype(jnp.bfloat16)
    grad_w_in = outer_sum(normed_ffn, grad_gate_up)
    grad_normed3 = back_product(grad_gate_up, w_in)
    grad_cross_state, grad_gain3 = norm_backward(after_cross, gains[2], grad_normed3)
    grad_cross_state = grad_cross_state + upstream
    ffn_sums = (
        lax.psum_scatter(
            grad_w_in.reshape(-1), ("wide", "narrow"), scatter_dimension=0, tiled=True
        ),
        lax.psum_scatter(
            grad_w_out3.reshape(-1), ("wide", "narrow"), scatter_dimension=0, tiled=True
        ),
    )
    grad_branch2 = grad_cross_state.astype(jnp.bfloat16)
    grad_w_out2 = outer_sum(cross_flat, grad_branch2)
    grad_cross_mixed = (
        back_product(grad_branch2, second_output_weight)
        .astype(jnp.bfloat16)
        .reshape(pair_count, seq_len, head_count, head_size)
    )

    def cross_backward(carry, pair_items):
        query_rows, memory_rows, key_values, lse_rows, grad_rows = pair_items
        keys_pair = key_values[:, :model_width].reshape(memory_len, head_count, head_size)
        values_pair = key_values[:, model_width:].reshape(memory_len, head_count, head_size)
        scores = (
            jnp.einsum("qhd,khd->hqk", query_rows, keys_pair, preferred_element_type=jnp.float32)
            * score_scale
        )
        probs = jnp.exp(scores - lse_rows)
        grad_values = jnp.einsum(
            "hqk,qhd->khd",
            probs.astype(jnp.bfloat16),
            grad_rows,
            preferred_element_type=jnp.float32,
        )
        grad_probs = jnp.einsum(
            "qhd,khd->hqk", grad_rows, values_pair, preferred_element_type=jnp.float32
        )
        grad_scores = (
            probs * (grad_probs - jnp.sum(grad_probs * probs, axis=-1, keepdims=True))
        ).astype(jnp.bfloat16)
        grad_queries = (
            jnp.einsum("hqk,khd->qhd", grad_scores, keys_pair, preferred_element_type=jnp.float32)
            * score_scale
        )
        grad_keys = (
            jnp.einsum("hqk,qhd->khd", grad_scores, query_rows, preferred_element_type=jnp.float32)
            * score_scale
        )
        grad_kv = jnp.concatenate(
            [
                grad_keys.reshape(memory_len, model_width),
                grad_values.reshape(memory_len, model_width),
            ],
            axis=1,
        ).astype(jnp.bfloat16)
        carry = carry + outer_sum(memory_rows, grad_kv)
        memory_rows_grad = back_product(grad_kv, w_kv2).astype(jnp.bfloat16)
        return (
            carry,
            (grad_queries.reshape(seq_len, model_width).astype(jnp.bfloat16), memory_rows_grad),
        )

    grad_w_kv2, (grad_cross_q, memory_grad) = lax.scan(
        cross_backward,
        jnp.zeros((model_width, 2 * model_width), jnp.float32),
        (cross_queries, memory, kept_kv, cross_lse, grad_cross_mixed),
    )
    grad_cross_flat = grad_cross_q.reshape(token_count, model_width)
    grad_w_q2 = outer_sum(normed_cross, grad_cross_flat)
    grad_normed2 = back_product(grad_cross_flat, w_q2)
    grad_self_state, grad_gain2 = norm_backward(after_self, gains[1], grad_normed2)
    grad_self_state = grad_self_state + grad_cross_state
    cross_sums = (
        lax.psum_scatter(
            grad_w_q2.reshape(-1), ("wide", "narrow"), scatter_dimension=0, tiled=True
        ),
        lax.psum_scatter(
            grad_w_kv2.reshape(-1), ("wide", "narrow"), scatter_dimension=0, tiled=True
        ),
        lax.psum_scatter(
            grad_w_out2.reshape(-1), ("wide", "narrow"), scatter_dimension=0, tiled=True
        ),
    )
    grad_branch1 = grad_self_state.astype(jnp.bfloat16)
    grad_w_out1 = outer_sum(self_mixed, grad_branch1)
    grad_self_mixed = (
        back_product(grad_branch1, w_out1)
        .astype(jnp.bfloat16)
        .reshape(pair_count, seq_len, head_count, head_size)
    )
    probs_again = jnp.exp(
        score_self(queries, keys_self, expanded_bias, allowed, score_scale) - self_lse
    )
    grad_values = jnp.einsum(
        "phqk,pqhd->pkhd",
        probs_again.astype(jnp.bfloat16),
        grad_self_mixed,
        preferred_element_type=jnp.float32,
    )
    grad_probs = jnp.einsum(
        "pqhd,pkhd->phqk", grad_self_mixed, values_self, preferred_element_type=jnp.float32
    )
    grad_scores = (
        probs_again * (grad_probs - jnp.sum(grad_probs * probs_again, axis=-1, keepdims=True))
    ).astype(jnp.bfloat16)
    grad_bias = jnp.einsum(
        "tud,gud->tg",
        bucket_indicator,
        jnp.sum(grad_scores, axis=0, dtype=jnp.float32),
        precision=top_precision,
    )
    grad_queries = (
        jnp.einsum("phqk,pkhd->pqhd", grad_scores, keys_self, preferred_element_type=jnp.float32)
        * score_scale
    )
    grad_keys = (
        jnp.einsum("phqk,pqhd->pkhd", grad_scores, queries, preferred_element_type=jnp.float32)
        * score_scale
    )
    grad_joined = (
        jnp.stack([grad_queries, grad_keys, grad_values], axis=2)
        .reshape(token_count, 3 * model_width)
        .astype(jnp.bfloat16)
    )
    grad_w_qkv = outer_sum(self_normalized, grad_joined)
    grad_first_normalized = back_product(grad_joined, w_qkv)
    grad_embedded, grad_gain1 = norm_backward(embedded, gains[0], grad_first_normalized)
    grad_embedded = grad_embedded + grad_self_state
    row_grads = grad_embedded * valid_flat
    slot_grads = (
        jnp.zeros((owner_count * capacity, model_width), jnp.float32).at[slot_index].set(row_grads)
    )
    returned = lax.all_to_all(
        lax.all_to_all(
            slot_grads.reshape(wide_count, narrow_count, capacity, model_width).astype(
                jnp.bfloat16
            ),
            "wide",
            split_axis=0,
            concat_axis=0,
            tiled=True,
        ),
        "narrow",
        split_axis=1,
        concat_axis=1,
        tiled=True,
    ).astype(jnp.float32)
    segment_ids = jnp.where(requests >= 0, requests, shard_rows).reshape(-1)
    table_grad = jax.ops.segment_sum(
        returned.reshape(-1, model_width), segment_ids, num_segments=shard_rows + 1
    )[:shard_rows]
    self_sums = (
        lax.psum_scatter(
            grad_w_qkv.reshape(-1), ("wide", "narrow"), scatter_dimension=0, tiled=True
        ),
        lax.psum_scatter(
            grad_w_out1.reshape(-1), ("wide", "narrow"), scatter_dimension=0, tiled=True
        ),
    )
    weight_sums = (
        self_sums[0],
        self_sums[1],
        cross_sums[0],
        cross_sums[1],
        cross_sums[2],
        ffn_sums[0],
        ffn_sums[1],
    )
    small_sums = lax.psum(
        (jnp.stack([grad_gain1, grad_gain2, grad_gain3]), grad_bias), ("wide", "narrow")
    )
    return (
        hidden,
        memory_grad,
        table_grad,
        weight_sums[0],
        weight_sums[1],
        weight_sums[2],
        weight_sums[3],
        weight_sums[4],
        weight_sums[5],
        weight_sums[6],
        small_sums[0],
        small_sums[1],
    )


def solution(mesh):
    return jax.shard_map(
        body,
        mesh=mesh,
        in_specs=(
            P(("wide", "narrow"), None),
            P(("wide", "narrow")),
            P(),
            P(("wide", "narrow"), None, None),
            P(("wide", "narrow"), None),
            P(("wide", "narrow")),
            P(("wide", "narrow")),
            P(("wide", "narrow")),
            P(("wide", "narrow")),
            P(("wide", "narrow")),
            P(("wide", "narrow")),
            P(("wide", "narrow")),
            P(),
            P(),
            P(("wide", "narrow"), None, None),
        ),
        out_specs=(
            P(("wide", "narrow"), None, None),
            P(("wide", "narrow"), None, None),
            P(("wide", "narrow"), None),
            P(("wide", "narrow")),
            P(("wide", "narrow")),
            P(("wide", "narrow")),
            P(("wide", "narrow")),
            P(("wide", "narrow")),
            P(("wide", "narrow")),
            P(("wide", "narrow")),
            P(),
            P(),
        ),
        check_vma=False,
    )
```

profile of v0, /device:TPU:0, one launch (start us, length us, event | category | flops | bytes accessed | tf_op | source)
XLA Modules:
  0.0 1177.5 jit_solution(1353083826765744607)
XLA Ops:
  15.6 13.6 %all_to_all.30 = s32[8,4,12]{2,1,0:T(4,128)S(1)} all-to-all(s32[8,4,12]{2,1,0:T(4,128)S(1)} %reshape.584), channel_id=1, replica_groups=mesh['wide'=8,'narrow'=4] {'wide'}, dimensions={0} | all-to-all | bytes 3072 | tf_op jit(solution)/shard_map/all_to_all | solution.py:121
  37.7 8.5 gather_fusion
  53.8 227.4 %gather_fusion.2 = s32[36864]{0:T(1024)S(1)} fusion(s32[192]{0:T(256)S(1)} %copy-done.1, s32[36864]{0:T(1024)S(1)} %broadcast_clamp_fusion), kind=kCustom, calls=%fused_computation.2 | custom fusion | bytes 442368 | tf_op jit(solution)/shard_map/jit(_take)/gather | solution.py:101
  292.9 7.2 all-to-all-done.3
  334.2 32.0 %all-gather.8.cloned.1.call-done = bf16[1769472]{0:T(1024)(128)(2,1)} async-done(((bf16[55296]{0:T(1024)(128)(2,1)}), bf16[1769472]{0:T(1024)(128)(2,1)}) %all-gather.8.cloned.1.call-update) | async-done | bytes 3538960 | tf_op jit(solution)/shard_map/all_gather | solution.py:149
  366.2 7.6 reshape.586
  390.4 9.2 multiply_reduce_fusion.1
  399.6 7.7 fusion
  407.3 6.9 fusion.35
  416.7 20.7 %all-gather.18.cloned.1.call-done = bf16[3145728]{0:T(1024)(128)(2,1)} async-done(((bf16[98304]{0:T(1024)(128)(2,1)}), bf16[3145728]{0:T(1024)(128)(2,1)}) %all-gather.18.cloned.1.call-update) | async-done | bytes 6291472 | tf_op jit(solution)/shard_map/all_gather | solution.py:154
  437.5 10.7 reshape.599
  471.4 9.4 fusion.11
  480.8 10.3 multiply_reduce_fusion
  491.2 7.3 multiply_convert_fusion
  528.2 7.1 reshape.613
  535.3 12.2 %copy.109 = f32[96,32,8,128]{3,1,2,0:T(8,128)} copy(f32[96,32,8,128]{3,2,1,0:T(8,128)} %convolution_bitcast_fusion) | data formatting | bytes 25165824
  547.5 7.7 convolution_bitcast_fusion.1
  580.1 7.9 reshape.607
  612.1 7.8 fusion.16
  619.9 10.8 all-to-all-done.4
  635.9 43.2 %all-reduce.8 = (f32[3,768]{1,0:T(4,128)}, f32[32,12]{0,1:T(8,128)}) all-reduce(f32[3,768]{1,0:T(4,128)S(1)} %pad_maximum_fusion.8, f32[32,12]{0,1:T(8,128)} %fusion.38), channel_id=1, replica_groups=mesh['wide'=8,'narrow'=4] {'wide','narrow'}, use_global_device_ids=true, to_apply=%region_28.29 | all-reduce | flops 2688 | bytes 21504 | tf_op jit(solution)/shard_map/psum | solution.py:404
  685.8 14.4 %scatter_custom_fusion.2 = f32[7817,768]{1,0:T(8,128)} fusion(s32[384]{0:T(512)} %reshape.662, f32[384,768]{1,0:T(8,128)S(1)} %reshape.664, f32[]{:T(128)} %constant.71.clone.1), kind=kCustom, calls=%fused_computation.12 | custom fusion | flops 294912 | bytes 24014336 | tf_op jit(solution)/shard_map/scatter-add | solution.py:384
  700.1 16.9 %slice.82 = f32[7816,768]{1,0:T(8,128)} slice(f32[7817,768]{1,0:T(8,128)} %scatter_custom_fusion.2), slice={[0:7816], [0:768]} | slice | bytes 48021504 | tf_op jit(solution)/shard_map/slice | solution.py:384
  717.1 442.0 %all-reduce.12.cloned.1.call-done = (f32[1769472]{0:T(1024)}, f32[589824]{0:T(1024)}, f32[589824]{0:T(1024)}, f32[1179648]{0:T(1024)}, f32[589824]{0:T(1024)}, /*index=5*/f32[3145728]{0:T(1024)}, f32[1572864]{0:T(1024)}) async-done(((f32[1769472]{0:T(1024)}, f32[589824]{0:T(1024)}, f32[589824]{0:T(1024)}, f32[1179648]{0:T(1024)}, f32[589824]{0:T(1024)}, /*index=5*/f32[3145728]{0:T(1024)}, ...) | async-done | bytes 37748752
  (271 shorter events, 212.7 us)
Async XLA Ops:
  7.2 312.3 %copy-start = (bf16[1,1536,768]{2,1,0:T(8,128)(2,1)S(1)}, bf16[1,1536,768]{2,1,0:T(8,128)(2,1)}, u32[]{:S(2)}) copy-start(bf16[1,1536,768]{2,1,0:T(8,128)(2,1)} %param.18) | copy-start | bytes 7077892
  7.2 296.6 %all-gather.10.cloned.1.call-start = ((), (), s32[]{:S(2)}) async-start(), calls=%async_computation.7 | async-start | bytes 1216512 | tf_op jit(solution)/shard_map/all_gather | solution.py:150
  7.9 299.3 %all-gather.14.cloned.1.call-start = ((), (), s32[]{:S(2)}) async-start(), calls=%async_computation.9 | async-start | bytes 1216512 | tf_op jit(solution)/shard_map/all_gather | solution.py:151
  8.7 301.9 %all-gather.16.cloned.1.call-start = ((), (), s32[]{:S(2)}) async-start(), calls=%async_computation.10 | async-start | bytes 1216512 | tf_op jit(solution)/shard_map/all_gather | solution.py:153
  9.4 304.5 %all-gather.12.cloned.1.call-start = ((), (), s32[]{:S(2)}) async-start(), calls=%async_computation.8 | async-start | bytes 2433024 | tf_op jit(solution)/shard_map/all_gather | solution.py:152
  10.0 317.8 %all-gather.20.cloned.1.call-start = ((), (), s32[]{:S(2)}) async-start(), calls=%async_computation.12 | async-start | bytes 3244032 | tf_op jit(solution)/shard_map/all_gather | solution.py:155
  10.6 355.6 %all-gather.8.cloned.1.call-start = ((), (), s32[]{:S(2)}) async-start(), calls=%async_computation.6 | async-start | bytes 3649536 | tf_op jit(solution)/shard_map/all_gather | solution.py:149
  11.2 426.3 %all-gather.18.cloned.1.call-start = ((), (), s32[]{:S(2)}) async-start(), calls=%async_computation.11 | async-start | bytes 6488064 | tf_op jit(solution)/shard_map/all_gather | solution.py:154
  14.3 267.1 %copy-start.54 = (s32[192,1]{0,1:T(1,128)}, s32[192,1]{0,1:T(1,128)S(1)}, u32[]{:S(2)}) copy-start(s32[192,1]{0,1:T(1,128)S(1)} %compare_select_fusion.2) | copy-start | bytes 2308
  29.8 7.1 all-to-all-start.1
  49.6 233.2 %all-to-all-start.2 = ((bf16[8,4,12,768]{3,1,2,0:T(4,128)(2,1)}), bf16[8,4,12,768]{3,1,2,0:T(4,128)(2,1)S(1)}, u32[]{:S(2)}, u32[]{:S(2)}) async-start(bf16[8,4,12,768]{3,1,2,0:T(4,128)(2,1)} %copy.84), calls=%async_computation.2 | async-start | bytes 1179648 | tf_op jit(solution)/shard_map/all_to_all | solution.py:137
  283.8 16.3 %all-to-all-start.3 = ((bf16[8,4,12,768]{3,0,2,1:T(8,128)(2,1)}), bf16[8,4,12,768]{3,0,2,1:T(8,128)(2,1)S(1)}, u32[]{:S(2)}, u32[]{:S(2)}) async-start(bf16[8,4,12,768]{3,0,2,1:T(8,128)(2,1)} %copy.85), calls=%async_computation.3 | async-start | bytes 1179648 | tf_op jit(solution)/shard_map/all_to_all | solution.py:136
  287.3 871.8 %all-reduce.12.cloned.1.call-start = ((), (), s32[]{:S(2)}) async-start(), calls=%async_computation.13 | async-start | bytes 75497472
  287.6 13.5 %copy-start.33 = (s32[192,192]{0,1:T(8,128)}, s32[192,192]{0,1:T(8,128)S(1)}, u32[]{:S(2)}) copy-start(s32[192,192]{0,1:T(8,128)S(1)} %copy.88) | copy-start | bytes 442372
  303.5 83.2 %copy-start.6 = (bf16[192,768]{1,0:T(8,128)(2,1)}, bf16[192,768]{1,0:T(8,128)(2,1)S(1)}, u32[]{:S(2)}) copy-start(bf16[192,768]{1,0:T(8,128)(2,1)S(1)} %gather_fusion.1) | copy-start | bytes 884740
  303.8 70.0 %copy-start.45 = (f32[192]{0:T(256)}, f32[192]{0:T(256)S(1)}, u32[]{:S(2)}) copy-start(f32[192]{0:T(256)S(1)} %fusion.79) | copy-start | bytes 2308
  471.4 9.4 copy-start.34
  471.4 19.8 %slice-start = ((s8[14155776]{0:T(1024)(128)(4,1)}), s8[4194304]{0:T(1024)(128)(4,1)S(1)}, s32[]{:S(2)}) async-start(s8[14155776]{0:T(1024)(128)(4,1)} %bitcast.160), calls=%async_computation.14 | async-start | bytes 8388608
  471.4 19.8 %slice-start.1 = ((s8[14155776]{0:T(1024)(128)(4,1)}), s8[4194304]{0:T(1024)(128)(4,1)S(1)}, s32[]{:S(2)}) async-start(s8[14155776]{0:T(1024)(128)(4,1)} %bitcast.160), calls=%async_computation.15 | async-start | bytes 8388608
  480.8 10.4 slice-start.2
  480.8 10.4 slice-start.3
  535.3 12.2 %copy-start.21 = (bf16[12,64,1536]{2,1,0:T(8,128)(2,1)S(1)}, bf16[12,64,1536]{2,1,0:T(8,128)(2,1)}, u32[]{:S(2)}) copy-start(bf16[12,64,1536]{2,1,0:T(8,128)(2,1)} %multiply_convert_fusion.1) | copy-start | bytes 7077892
  604.3 26.4 %all-to-all-start.4 = ((bf16[8,4,12,768]{3,1,2,0:T(4,128)(2,1)}), bf16[8,4,12,768]{3,1,2,0:T(4,128)(2,1)S(1)}, u32[]{:S(2)}, u32[]{:S(2)}) async-start(bf16[8,4,12,768]{3,1,2,0:T(4,128)(2,1)} %copy.98), calls=%async_computation.4 | async-start | bytes 1179648 | tf_op jit(solution)/shard_map/all_to_all | solution.py:369
  631.7 51.2 %all-to-all-start.5 = ((bf16[8,4,12,768]{3,0,2,1:T(8,128)(2,1)}), bf16[8,4,12,768]{3,0,2,1:T(8,128)(2,1)S(1)}, u32[]{:S(2)}, u32[]{:S(2)}) async-start(bf16[8,4,12,768]{3,0,2,1:T(8,128)(2,1)} %copy.99), calls=%async_computation.5 | async-start | bytes 1179648 | tf_op jit(solution)/shard_map/all_to_all | solution.py:368
  (51 other events, 165.7 us)
Sparse Core Ops, SparseCore 0:
  10.9 61.6 all-gather.9
  75.6 51.3 all-gather.13
  129.9 53.0 all-gather.15
  185.8 56.1 all-gather.11
  244.8 59.4 all-gather.19
  307.1 59.0 all-gather.7
  369.1 68.3 all-gather.17
  588.2 570.8 all-reduce.11
where the time goes:
time: 1190 us; the launch traced here: 1180 us
  waiting for transfers between devices  521 us (44%)
  local copies, waits for them, and re-layouts  386 us (32%)
  matrix products  134 us (11%)
  blocking collectives  56.9 us (5%)
  other arithmetic  45.1 us (4%)
  starting transfers between devices  18 us (2%)
  between operations  16.1 us (1%)
    unnamed x9, waiting for transfers between devices  446 us
    gather x2, local copies, waits for them, and re-layouts, body(): bucket_ids = jnp.take(bucket_table, distance)  228 us
    psum x1, blocking collectives, body(): lax.psum((jnp.stack([grad_gain1, grad_gain2, grad_gain3]), grad_bias), ('...  43.2 us
    all_gather x1, waiting for transfers between devices, body(): lax.all_gather(shards[0], ('wide', 'narrow'), axis=0, tiled=True)  32 us
    dot_general x7, matrix products, outer_sum(): lax.dot_general(left, right, (((0,), (0,)), ((), ())), preferred_element_...  29.1 us
    unnamed x132, local copies, waits for them, and re-layouts  28 us
  transfers between devices with their start and end apart: 13, of which 6 were waited for; matrix products, arithmetic and copies ran while one was open for 34% of the time, Pallas kernels for 0%

commit v1 on v0

v1 whole, which is shorter than its diff:
```python
import functools

import jax
import jax.numpy as jnp
from jax import lax
from jax.experimental import pallas as pl
from jax.experimental.pallas import tpu as pltpu
from jax.sharding import PartitionSpec as P

epsilon = 1e-06
blocked = -1e30
top_precision = lax.Precision.HIGHEST
axes = ("wide", "narrow")
bf16 = jnp.bfloat16
f32 = jnp.float32


def rms_scaled(inputs, gain):
    return inputs * lax.rsqrt(jnp.mean(inputs * inputs, axis=-1, keepdims=True) + epsilon) * gain


def norm_backward(inputs, gain, upstream):
    unused, pullback = jax.vjp(rms_scaled, inputs, gain)
    return pullback(upstream)


def gated(gate, upper):
    return jax.nn.gelu(gate, approximate=True) * upper


def matmul(left, right):
    return jnp.dot(left, right, preferred_element_type=f32)


def outer_sum(left, right):
    return lax.dot_general(left, right, (((0,), (0,)), ((), ())), preferred_element_type=f32)


def back_product(left, right):
    return lax.dot_general(left, right, (((1,), (1,)), ((), ())), preferred_element_type=f32)


mesh_ids = pl.DeviceIdType.MESH
roomy = pltpu.CompilerParams(vmem_limit_bytes=48 * 1024 * 1024)


def standing():
    wide, narrow = lax.axis_index("wide"), lax.axis_index("narrow")
    return wide // 2, wide % 2, narrow // 2, narrow % 2


def device_at(z, x, y, core):
    return (z * 2 + x, y * 2 + core)


def flips(x, y, core):
    far_x, far_y = 1 - x, 1 - y
    second = (x * (1 - core) + far_x * core, far_y * (1 - core) + y * core)
    first = (far_x * (1 - core) + x * core, y * (1 - core) + far_y * core)
    return ((x, y), second, first, (far_x, far_y))


def partners():
    z, x, y, core = standing()
    own, second, first, both = flips(x, y, core)
    along_z = [device_at((z + step) % 4, x, y, core) for step in (1, 2, 3)]
    return along_z, device_at(z, *second, core), device_at(z, *first, core), device_at(z, x, y, 1 - core)


def greet(devices):
    barrier = pltpu.get_barrier_semaphore()
    for device in devices:
        pl.semaphore_signal(barrier, inc=1, device_id=device, device_id_type=mesh_ids)
    pl.semaphore_wait(barrier, len(devices))


def remote(source, target, send_sem, recv_sem, index, device):
    return pltpu.make_async_remote_copy(
        src_ref=source,
        dst_ref=target,
        send_sem=send_sem.at[index],
        recv_sem=recv_sem.at[index],
        device_id=device,
        device_id_type=mesh_ids,
    )


def gather_kernel(count, *refs):
    shards, outs = refs[:count], refs[count:2 * count]
    send_sem, recv_sem, own_sem = refs[2 * count:]
    z, x, y, core = standing()
    sets = flips(x, y, core)
    along_z, second, first, sibling = partners()
    greet(along_z + [second, first, sibling])
    own_copies = []
    for chunk in range(count):
        own = pltpu.make_async_copy(
            shards[chunk], outs[chunk].at[z, x, y, core], own_sem.at[chunk]
        )
        own.start()
        own_copies.append(own)

    def stage(number, chunk):
        base = chunk * 10
        out = outs[chunk]
        if number == 0:
            return [
                remote(shards[chunk], out.at[z, x, y, core], send_sem, recv_sem, base + k, device)
                for k, device in enumerate(along_z)
            ]
        piece = lambda k: out.at[:, sets[k][0], sets[k][1], core]
        copies = []
        device = (second, first, sibling)[number - 1]
        amount = (1, 2, 4)[number - 1]
        for k in range(amount):
            copies.append(
                remote(piece(k), piece(k), send_sem, recv_sem, base + 2 + amount + k, device)
            )
        return copies

    flying = {}
    for step in range(count + 4):
        for number in (3, 2, 1, 0):
            chunk = step - number
            if 0 <= chunk < count:
                if number == 1:
                    own_copies[chunk].wait()
                if number > 0:
                    for copy in flying[number - 1, chunk]:
                        copy.wait_recv()
                flying[number, chunk] = stage(number, chunk)
                for copy in flying[number, chunk]:
                    copy.start()
        chunk = step - 4
        if chunk >= 0:
            for copy in flying[3, chunk]:
                copy.wait_recv()
    for copies in flying.values():
        for copy in copies:
            copy.wait_send()


def gather_weights(shards, special):
    if not special:
        return [lax.all_gather(shard, axes, axis=0, tiled=True) for shard in shards]
    count = len(shards)
    outs = pl.pallas_call(
        functools.partial(gather_kernel, count),
        out_shape=[jax.ShapeDtypeStruct((4, 2, 2, 2) + shard.shape, bf16) for shard in shards],
        in_specs=[pl.BlockSpec(memory_space=pltpu.VMEM)] * count,
        out_specs=[pl.BlockSpec(memory_space=pl.ANY)] * count,
        scratch_shapes=[
            pltpu.SemaphoreType.DMA((10 * count,)),
            pltpu.SemaphoreType.DMA((10 * count,)),
            pltpu.SemaphoreType.DMA((count,)),
        ],
        compiler_params=pltpu.CompilerParams(
            collective_id=1, has_side_effects=True, vmem_limit_bytes=48 * 1024 * 1024
        ),
    )(*shards)
    return [out.reshape(-1, out.shape[-1]) for out in outs]


def add_into(target, source):
    def quarter(index, unused):
        target[index] = (target[index].astype(f32) + source[index].astype(f32)).astype(bf16)
        return unused

    lax.fori_loop(0, 4, quarter, 0)


def reduce_kernel(count, *refs):
    grads, small = refs[:count], refs[count]
    outs, small_out = refs[count + 1:2 * count + 1], refs[2 * count + 1]
    scratch = refs[2 * count + 2:]
    kept, from_core, from_first, from_second, from_z = [
        scratch[k * count:(k + 1) * count] for k in range(5)
    ]
    small_in, send_sem, recv_sem, load_sem, small_send, small_recv = scratch[5 * count:]
    z, x, y, core = standing()
    sets = flips(x, y, core)
    sibling_sets = flips(x, y, 1 - core)
    along_z, second, first, sibling = partners()
    greet(along_z + [second, first, sibling])
    small_out[...] = small[...]

    loads = {}

    def stage(number, chunk):
        base = chunk * 10
        if number == 0:
            loads[chunk] = [
                pltpu.make_async_copy(
                    grads[chunk].at[:, sets[k][0], sets[k][1], core],
                    kept[chunk].at[k],
                    load_sem.at[4 * chunk + k],
                )
                for k in range(4)
            ]
            return [
                remote(
                    grads[chunk].at[:, sibling_sets[k][0], sibling_sets[k][1], 1 - core],
                    from_core[chunk].at[k],
                    send_sem,
                    recv_sem,
                    base + k,
                    sibling,
                )
                for k in range(4)
            ]
        if number == 1:
            return [
                remote(
                    kept[chunk].at[2 + k],
                    from_first[chunk].at[k],
                    send_sem,
                    recv_sem,
                    base + 4 + k,
                    first,
                )
                for k in range(2)
            ]
        if number == 2:
            return [
                remote(kept[chunk].at[1], from_second[chunk], send_sem, recv_sem, base + 6, second)
            ]
        return [
            remote(
                kept[chunk].at[0, (z + k + 1) % 4],
                from_z[chunk].at[k],
                send_sem,
                recv_sem,
                base + 7 + k,
                along_z[k],
            )
            for k in range(3)
        ]

    def settle(number, chunk):
        for copy in flying[number, chunk]:
            copy.wait_recv()
        if number == 0:
            for load in loads[chunk]:
                load.wait()
            for k in (2, 3, 1, 0):
                add_into(kept[chunk].at[k], from_core[chunk].at[k])
        elif number == 1:
            for k in (1, 0):
                add_into(kept[chunk].at[k], from_first[chunk].at[k])
        elif number == 2:
            add_into(kept[chunk].at[0], from_second[chunk])
        else:
            total = kept[chunk][0, z].astype(f32)
            for k in range(3):
                total = total + from_z[chunk][k].astype(f32)
            outs[chunk][...] = total

    flying = {}
    for step in range(count + 4):
        for number in (4, 3, 2, 1, 0):
            chunk = step - number
            if 0 <= chunk < count:
                if number > 0:
                    settle(number - 1, chunk)
                if number < 4:
                    flying[number, chunk] = stage(number, chunk)
                    for copy in flying[number, chunk] + (loads[chunk] if number == 0 else []):
                        copy.start()
        if step == 0:
            number = 0
            for group in ([sibling], [first], [second], along_z):
                copies = []
                for device in group:
                    copies.append(
                        remote(small_out, small_in.at[number], small_send, small_recv, number, device)
                    )
                    number += 1
                for copy in copies:
                    copy.start()
                for copy in copies:
                    copy.wait()
                total = small_out[...]
                for index in range(number - len(group), number):
                    total = total + small_in[index]
                small_out[...] = total
    for copies in flying.values():
        for copy in copies:
            copy.wait_send()


def reduce_grads(grads, small, special):
    if not special:
        sums = [lax.psum_scatter(grad, axes, scatter_dimension=0, tiled=True) for grad in grads]
        return [total.astype(f32) for total in sums], lax.psum(small, axes)
    count = len(grads)
    grads = [grad.reshape(4, 2, 2, 2, -1, grad.shape[-1]) for grad in grads]
    shapes = [grad.shape[4:] for grad in grads]
    several = lambda *lead: [pltpu.VMEM(lead + shape, bf16) for shape in shapes]
    results = pl.pallas_call(
        functools.partial(reduce_kernel, count),
        out_shape=[jax.ShapeDtypeStruct(shape, f32) for shape in shapes]
        + [jax.ShapeDtypeStruct(small.shape, f32)],
        in_specs=[pl.BlockSpec(memory_space=pl.ANY)] * count
        + [pl.BlockSpec(memory_space=pltpu.VMEM)],
        out_specs=[pl.BlockSpec(memory_space=pltpu.VMEM)] * (count + 1),
        scratch_shapes=several(4, 4)
        + several(4, 4)
        + several(2, 4)
        + several(4)
        + several(3)
        + [
            pltpu.VMEM((6,) + small.shape, f32),
            pltpu.SemaphoreType.DMA((10 * count,)),
            pltpu.SemaphoreType.DMA((10 * count,)),
            pltpu.SemaphoreType.DMA((4 * count,)),
            pltpu.SemaphoreType.DMA((6,)),
            pltpu.SemaphoreType.DMA((6,)),
        ],
        compiler_params=pltpu.CompilerParams(
            collective_id=2, has_side_effects=True, vmem_limit_bytes=60 * 1024 * 1024
        ),
    )(*grads, small)
    return results[:count], results[count]


def spread_heads(pair, head_size):
    lane = lax.broadcasted_iota(jnp.int32, pair.shape, 1)
    zero = jnp.zeros_like(pair)
    return jnp.concatenate(
        [jnp.where(lane < head_size, pair, zero), jnp.where(lane >= head_size, pair, zero)], axis=0
    )


def join_heads(spread, head_size):
    turned = spread.T
    rows = turned.shape[0] // 2
    lane = lax.broadcasted_iota(jnp.int32, (rows, turned.shape[1]), 1)
    return jnp.where(lane < head_size, turned[:rows], turned[rows:])


def down_product(left, right):
    return lax.dot_general(left, right, (((0,), (0,)), ((), ())), preferred_element_type=f32)


def column_softmax(scores):
    peak = jnp.max(scores, axis=0, keepdims=True)
    exponent = jnp.exp(scores - peak)
    return exponent / jnp.sum(exponent, axis=0, keepdims=True)


def self_forward_kernel(head_size, q_ref, k_ref, v_ref, bias_ref, keep_ref, out_ref, prob_ref):
    scale = head_size ** (-0.5)
    scores = back_product(k_ref[...], spread_heads(q_ref[...], head_size)) * scale
    length, both = scores.shape
    row = lax.broadcasted_iota(jnp.int32, scores.shape, 0)
    lane = lax.broadcasted_iota(jnp.int32, scores.shape, 1)
    query = jnp.where(lane >= length, lane - length, lane)
    bias = pltpu.roll(
        jnp.broadcast_to(bias_ref[0], scores.shape), 0, 1, stride=1, stride_axis=0
    )
    scores = jnp.where((row <= query) & (keep_ref[...] > 0.0), scores + bias, blocked)
    probs = column_softmax(scores).astype(bf16)
    prob_ref[0] = probs
    out_ref[...] = join_heads(down_product(v_ref[...], probs), head_size).astype(bf16)


def self_backward_kernel(
    head_size, q_ref, k_ref, v_ref, prob_ref, grad_ref, out_ref, bias_ref
):
    scale = head_size ** (-0.5)
    pair = pl.program_id(0)
    width = 2 * head_size
    model = out_ref.shape[1] // 3
    grad = spread_heads(grad_ref[...], head_size)
    probs = prob_ref[0]
    wide_probs = probs.astype(f32)
    grad_probs = back_product(v_ref[...], grad)
    center = jnp.sum(grad_probs * wide_probs, axis=0, keepdims=True)
    grad_scores = (wide_probs * (grad_probs - center)).astype(bf16)
    grad_value = matmul(probs, grad)
    grad_key = matmul(grad_scores, spread_heads(q_ref[...], head_size)) * scale
    grad_query = join_heads(down_product(k_ref[...], grad_scores), head_size) * scale
    out_ref[:, pl.ds(pl.multiple_of(pair * width, width), width)] = grad_query.astype(bf16)
    out_ref[:, pl.ds(pl.multiple_of(model + pair * width, width), width)] = grad_key.astype(bf16)
    out_ref[:, pl.ds(pl.multiple_of(2 * model + pair * width, width), width)] = grad_value.astype(
        bf16
    )
    folded = grad_scores.astype(f32)
    both = folded.shape[1]
    while folded.shape[0] % 16 == 0:
        rows = folded.shape[0] // 2
        folded = folded[:rows] + pltpu.roll(folded[rows:], both - rows, 1)
    total = folded[:8]
    for start in range(8, folded.shape[0], 8):
        total = total + pltpu.roll(folded[start:start + 8], both - start, 1)
    row = lax.broadcasted_iota(jnp.int32, total.shape, 0)
    for bit in (1, 2, 4):
        total = jnp.where((row // bit) % 2 == 1, pltpu.roll(total, both - bit, 1), total)
    bias_ref[0] = jnp.sum(total, axis=0, keepdims=True)


def cross_forward_kernel(head_size, q_ref, k_ref, v_ref, out_ref, prob_ref):
    scale = head_size ** (-0.5)
    scores = back_product(k_ref[...], spread_heads(q_ref[...], head_size)) * scale
    probs = column_softmax(scores).astype(bf16)
    prob_ref[0] = probs
    out_ref[...] = join_heads(down_product(v_ref[...], probs), head_size).astype(bf16)


def cross_backward_kernel(head_size, q_ref, k_ref, v_ref, prob_ref, grad_ref, out_ref, kv_ref):
    scale = head_size ** (-0.5)
    pair = pl.program_id(0)
    width = 2 * head_size
    model = kv_ref.shape[1] // 2
    grad = spread_heads(grad_ref[...], head_size)
    probs = prob_ref[0]
    wide_probs = probs.astype(f32)
    grad_probs = back_product(v_ref[...], grad)
    center = jnp.sum(grad_probs * wide_probs, axis=0, keepdims=True)
    grad_scores = (wide_probs * (grad_probs - center)).astype(bf16)
    grad_value = matmul(probs, grad)
    grad_key = matmul(grad_scores, spread_heads(q_ref[...], head_size)) * scale
    grad_query = join_heads(down_product(k_ref[...], grad_scores), head_size) * scale
    out_ref[...] = grad_query.astype(bf16)
    kv_ref[:, pl.ds(pl.multiple_of(pair * width, width), width)] = grad_key.astype(bf16)
    kv_ref[:, pl.ds(pl.multiple_of(model + pair * width, width), width)] = grad_value.astype(bf16)


def self_forward(merged, bias_rows, keep_rows, head_size):
    length, model = merged.shape[0], merged.shape[1] // 3
    width, pairs = 2 * head_size, model // (2 * head_size)
    both = 2 * length
    part = lambda offset: pl.BlockSpec((length, width), lambda p: (0, p + offset))
    return pl.pallas_call(
        functools.partial(self_forward_kernel, head_size),
        grid=(pairs,),
        out_shape=(
            jax.ShapeDtypeStruct((length, model), bf16),
            jax.ShapeDtypeStruct((pairs, length, both), bf16),
        ),
        in_specs=[
            part(0),
            part(pairs),
            part(2 * pairs),
            pl.BlockSpec((1, 1, both), lambda p: (p, 0, 0)),
            pl.BlockSpec((length, 1), lambda p: (0, 0)),
        ],
        out_specs=(part(0), pl.BlockSpec((1, length, both), lambda p: (p, 0, 0))),
        compiler_params=roomy,
        cost_estimate=pl.CostEstimate(flops=10**9, bytes_accessed=4 * 10**6, transcendentals=10**6),
    )(merged, merged, merged, bias_rows, keep_rows)


def self_backward(merged, probs, grad, head_size):
    length, model = grad.shape
    width, pairs = 2 * head_size, model // (2 * head_size)
    both = 2 * length
    part = lambda offset: pl.BlockSpec((length, width), lambda p: (0, p + offset))
    return pl.pallas_call(
        functools.partial(self_backward_kernel, head_size),
        grid=(pairs,),
        out_shape=(
            jax.ShapeDtypeStruct((length, 3 * model), bf16),
            jax.ShapeDtypeStruct((pairs, 1, both), f32),
        ),
        in_specs=[
            part(0),
            part(pairs),
            part(2 * pairs),
            pl.BlockSpec((1, length, both), lambda p: (p, 0, 0)),
            part(0),
        ],
        out_specs=(
            pl.BlockSpec((length, 3 * model), lambda p: (0, 0)),
            pl.BlockSpec((1, 1, both), lambda p: (p, 0, 0)),
        ),
        compiler_params=roomy,
        cost_estimate=pl.CostEstimate(flops=10**9, bytes_accessed=4 * 10**6, transcendentals=0),
    )(merged, merged, merged, probs, grad)


def cross_forward(queries, key_values, head_size):
    length, model = queries.shape
    memory_len = key_values.shape[0]
    width, pairs = 2 * head_size, model // (2 * head_size)
    both = 2 * length
    part = pl.BlockSpec((length, width), lambda p: (0, p))
    long_part = lambda offset: pl.BlockSpec((memory_len, width), lambda p: (0, p + offset))
    return pl.pallas_call(
        functools.partial(cross_forward_kernel, head_size),
        grid=(pairs,),
        out_shape=(
            jax.ShapeDtypeStruct((length, model), bf16),
            jax.ShapeDtypeStruct((pairs, memory_len, both), bf16),
        ),
        in_specs=[part, long_part(0), long_part(pairs)],
        out_specs=(part, pl.BlockSpec((1, memory_len, both), lambda p: (p, 0, 0))),
        compiler_params=roomy,
        cost_estimate=pl.CostEstimate(
            flops=4 * 10**9, bytes_accessed=13 * 10**6, transcendentals=4 * 10**6
        ),
    )(queries, key_values, key_values)


def cross_backward(queries, key_values, probs, grad, head_size):
    length, model = queries.shape
    memory_len = key_values.shape[0]
    width, pairs = 2 * head_size, model // (2 * head_size)
    both = 2 * length
    part = pl.BlockSpec((length, width), lambda p: (0, p))
    long_part = lambda offset: pl.BlockSpec((memory_len, width), lambda p: (0, p + offset))
    return pl.pallas_call(
        functools.partial(cross_backward_kernel, head_size),
        grid=(pairs,),
        out_shape=(
            jax.ShapeDtypeStruct((length, model), bf16),
            jax.ShapeDtypeStruct((memory_len, 2 * model), bf16),
        ),
        in_specs=[
            part,
            long_part(0),
            long_part(pairs),
            pl.BlockSpec((1, memory_len, both), lambda p: (p, 0, 0)),
            part,
        ],
        out_specs=(part, pl.BlockSpec((memory_len, 2 * model), lambda p: (0, 0))),
        compiler_params=roomy,
        cost_estimate=pl.CostEstimate(
            flops=8 * 10**9, bytes_accessed=18 * 10**6, transcendentals=0
        ),
    )(queries, key_values, key_values, probs, grad)


def body(
    target_ids,
    target_lengths,
    bucket_table,
    memory,
    table,
    self_qkv,
    self_out,
    cross_q,
    cross_kv,
    cross_out,
    ffn_in,
    ffn_out,
    gains,
    relative_bias,
    cotangent,
):
    pair_count, seq_len = target_ids.shape
    model_width = table.shape[1]
    bucket_count, head_count = relative_bias.shape
    head_size = model_width // head_count
    memory_len = memory.shape[1]
    wide_count = lax.axis_size("wide")
    narrow_count = lax.axis_size("narrow")
    owner_count = wide_count * narrow_count
    special = wide_count == 8 and narrow_count == 4
    ffn_width = ffn_out.shape[0] * owner_count // model_width
    token_count = pair_count * seq_len
    shard_rows = table.shape[0]
    capacity = max(2, (2 * token_count + owner_count - 1) // owner_count)
    slots = owner_count * capacity

    shards = [
        cross_kv.reshape(-1, 2 * model_width),
        self_qkv.reshape(-1, 3 * model_width),
        self_out.reshape(-1, model_width),
        cross_q.reshape(-1, model_width),
        cross_out.reshape(-1, model_width),
        *jnp.split(ffn_in.reshape(-1, 2 * ffn_width), 2, axis=1),
        ffn_out.reshape(-1, model_width),
    ]
    w_kv2, w_qkv, w_out1, w_q2, w_out2, w_gate, w_upper, w_out3 = gather_weights(shards, special)

    positions = jnp.arange(seq_len, dtype=jnp.int32)
    valid_flat = (positions[:, None] < target_lengths[0]).astype(f32)
    bucket_hits = (
        bucket_table[:, None] == jnp.arange(bucket_count, dtype=jnp.int32)[None, :]
    ).astype(f32)
    bias_rows = jnp.dot(relative_bias.T, bucket_hits.T, precision=top_precision).reshape(
        head_count // 2, 1, 2 * seq_len
    )

    flat_ids = target_ids.reshape(token_count)
    owner_index = flat_ids // shard_rows
    owner_hits = (owner_index[:, None] == jnp.arange(owner_count, dtype=jnp.int32)[None, :]).astype(
        jnp.int32
    )
    rank_within = jnp.sum(jnp.cumsum(owner_hits, axis=0) * owner_hits, axis=1) - 1
    slot_index = owner_index * capacity + rank_within
    slot_hits = slot_index[:, None] == jnp.arange(slots, dtype=jnp.int32)[None, :]
    outgoing = (
        jnp.sum(
            jnp.where(slot_hits, (flat_ids - owner_index * shard_rows + 1)[:, None], 0), axis=0
        )
        - 1
    )
    requests = lax.all_to_all(
        lax.all_to_all(
            outgoing.reshape(wide_count, narrow_count, capacity),
            "wide",
            split_axis=0,
            concat_axis=0,
            tiled=True,
        ),
        "narrow",
        split_axis=1,
        concat_axis=1,
        tiled=True,
    )
    found = table[jnp.maximum(requests, 0)]
    arrived = lax.all_to_all(
        lax.all_to_all(found, "wide", split_axis=0, concat_axis=0, tiled=True),
        "narrow",
        split_axis=1,
        concat_axis=1,
        tiled=True,
    ).reshape(slots, model_width)
    slot_pick = (slot_hits & (valid_flat > 0.0)).astype(bf16)
    embedded = matmul(slot_pick, arrived)

    memory_rows = memory.reshape(memory_len, model_width)
    key_values = matmul(memory_rows, w_kv2).astype(bf16)

    self_normalized = rms_scaled(embedded, gains[0]).astype(bf16)
    merged = matmul(self_normalized, w_qkv).astype(bf16)
    self_mixed, self_probs = self_forward(merged, bias_rows, valid_flat, head_size)
    after_self = embedded + matmul(self_mixed, w_out1)
    normed_cross = rms_scaled(after_self, gains[1]).astype(bf16)
    cross_queries = matmul(normed_cross, w_q2).astype(bf16)
    cross_mixed, cross_probs = cross_forward(cross_queries, key_values, head_size)
    after_cross = after_self + matmul(cross_mixed, w_out2)
    normed_ffn = rms_scaled(after_cross, gains[2]).astype(bf16)
    gate, upper = matmul(normed_ffn, w_gate), matmul(normed_ffn, w_upper)
    activated = gated(gate, upper).astype(bf16)
    hidden = (after_cross + matmul(activated, w_out3)) * valid_flat

    upstream = cotangent.reshape(token_count, model_width) * valid_flat
    grad_branch3 = upstream.astype(bf16)
    share_out3 = outer_sum(activated, grad_branch3).astype(bf16)
    grad_act = back_product(grad_branch3, w_out3)
    unused, gate_pull = jax.vjp(gated, gate, upper)
    grad_gate, grad_upper = [part.astype(bf16) for part in gate_pull(grad_act)]
    share_gate = outer_sum(normed_ffn, grad_gate).astype(bf16)
    share_upper = outer_sum(normed_ffn, grad_upper).astype(bf16)
    grad_normed3 = back_product(grad_gate, w_gate) + back_product(grad_upper, w_upper)
    grad_cross_state, grad_gain3 = norm_backward(after_cross, gains[2], grad_normed3)
    grad_cross_state = grad_cross_state + upstream

    grad_branch2 = grad_cross_state.astype(bf16)
    share_out2 = outer_sum(cross_mixed, grad_branch2).astype(bf16)
    grad_cross_mixed = back_product(grad_branch2, w_out2).astype(bf16)
    grad_cross_q, grad_kv = cross_backward(
        cross_queries, key_values, cross_probs, grad_cross_mixed, head_size
    )
    share_kv2 = outer_sum(memory_rows, grad_kv).astype(bf16)
    share_q2 = outer_sum(normed_cross, grad_cross_q).astype(bf16)
    grad_normed2 = back_product(grad_cross_q, w_q2)
    grad_self_state, grad_gain2 = norm_backward(after_self, gains[1], grad_normed2)
    grad_self_state = grad_self_state + grad_cross_state

    grad_branch1 = grad_self_state.astype(bf16)
    share_out1 = outer_sum(self_mixed, grad_branch1).astype(bf16)
    grad_self_mixed = back_product(grad_branch1, w_out1).astype(bf16)
    grad_joined, grad_distance = self_backward(merged, self_probs, grad_self_mixed, head_size)
    share_qkv = outer_sum(self_normalized, grad_joined).astype(bf16)
    grad_bias = jnp.dot(
        bucket_hits.T, grad_distance.reshape(head_count, seq_len).T, precision=top_precision
    )
    grad_first_normalized = back_product(grad_joined, w_qkv)
    grad_embedded, grad_gain1 = norm_backward(embedded, gains[0], grad_first_normalized)
    row_grads = (grad_embedded + grad_self_state).astype(bf16)
    slot_grads = outer_sum(slot_pick, row_grads).astype(bf16)
    returned = lax.all_to_all(
        lax.all_to_all(
            slot_grads.reshape(wide_count, narrow_count, capacity, model_width),
            "wide",
            split_axis=0,
            concat_axis=0,
            tiled=True,
        ),
        "narrow",
        split_axis=1,
        concat_axis=1,
        tiled=True,
    ).reshape(slots, model_width)
    row_hits = (
        jnp.arange(shard_rows, dtype=jnp.int32)[:, None] == requests.reshape(1, slots)
    ).astype(bf16)
    table_grad = matmul(row_hits, returned)
    memory_grad = back_product(grad_kv, w_kv2).astype(bf16)

    small = jnp.concatenate(
        [grad_gain1, grad_gain2, grad_gain3, grad_bias.reshape(-1)]
    )
    small_rows = -(-small.shape[0] // 1024) * 8
    small = jnp.pad(small, (0, small_rows * 128 - small.shape[0])).reshape(small_rows, 128)
    sums, small_sum = reduce_grads(
        [
            share_out3,
            share_gate,
            share_upper,
            share_kv2,
            share_out2,
            share_q2,
            share_out1,
            share_qkv,
        ],
        small,
        special,
    )
    sum_out3, sum_gate, sum_upper, sum_kv2, sum_out2, sum_q2, sum_out1, sum_qkv = sums
    small_sum = small_sum.reshape(-1)
    gain_count = 3 * model_width
    return (
        hidden.reshape(pair_count, seq_len, model_width),
        memory_grad.reshape(pair_count, memory_len, model_width),
        table_grad,
        sum_qkv.reshape(-1),
        sum_out1.reshape(-1),
        sum_q2.reshape(-1),
        sum_kv2.reshape(-1),
        sum_out2.reshape(-1),
        jnp.concatenate([sum_gate, sum_upper], axis=1).reshape(-1),
        sum_out3.reshape(-1),
        small_sum[:gain_count].reshape(3, model_width),
        small_sum[gain_count:gain_count + bucket_count * head_count].reshape(
            bucket_count, head_count
        ),
    )


def solution(mesh):
    split = P(axes)
    return jax.shard_map(
        body,
        mesh=mesh,
        in_specs=(
            P(axes, None),
            split,
            P(),
            P(axes, None, None),
            P(axes, None),
            split,
            split,
            split,
            split,
            split,
            split,
            split,
            P(),
            P(),
            P(axes, None, None),
        ),
        out_specs=(
            P(axes, None, None),
            P(axes, None, None),
            P(axes, None),
            split,
            split,
            split,
            split,
            split,
            split,
            split,
            P(),
            P(),
        ),
        check_vma=False,
    )
```

time: 1190 us -> 485 us (0.41)
  waiting for transfers between devices: 521 us -> 8.74 us
  local copies, waits for them, and re-layouts: 386 us -> 69.3 us
  Pallas kernels: 0 us -> 274 us
  matrix products: 134 us -> 79 us
  blocking collectives: 56.9 us -> 13.6 us
  other arithmetic: 45.1 us -> 5.89 us
  between operations: 16.1 us -> 2.42 us
    unnamed x9 -> x0, waiting for transfers between devices: 446 us -> none
    pallas_call x0 -> x6, Pallas kernels: none -> 274 us  [the longest x1 121 us: reduce_grads(): pl.pallas_call(functools.partial(reduce_kernel, count), out_shape=[jax.Sh...]
    gather x5 -> x3, local copies, waits for them, and re-layouts: 238 us -> 11.7 us  [body(): found = table[jnp.maximum(requests, 0)]]
    all_gather x7 -> x0, waiting for transfers between devices: 52.8 us -> none  [the longest x1 32 us: body(): lax.all_gather(shards[0], ('wide', 'narrow'), axis=0, tiled=True)]
    dot_general x21 -> x12, matrix products: 82.5 us -> 32.6 us  [the longest x10 31.4 us: matmul(): return jnp.dot(left, right, preferred_element_type=f32)]
    reshape x20 -> x22, local copies, waits for them, and re-layouts: 76.7 us -> 30 us  [the longest x2 4.36 us: body(): slot_grads.reshape(wide_count, narrow_count, capacity, model_width)]
    psum x1 -> x0, blocking collectives: 43.2 us -> none  [body(): lax.psum((jnp.stack([grad_gain1, grad_gain2, grad_gain3]), grad_bias), ('...]
    slice x3, local copies, waits for them, and re-layouts: 20.2 us -> 2.29 us  [the longest x1 1.44 us: body(): normed_ffn = rms_scaled(after_cross, gains[2]).astype(bf16)]
  transfers between devices with their start and end apart: 13 -> 5, of which waited for: 6 -> 2; matrix products, arithmetic and copies ran while one was open for 34% -> 11% of each run, Pallas kernels for 0% -> 50%
where the time goes in v1:
time: 485 us; the launch traced here: 477 us
  Pallas kernels  274 us (56%)
  matrix products  79 us (16%)
  local copies, waits for them, and re-layouts  69.3 us (14%)
  starting transfers between devices  24.6 us (5%)
  blocking collectives  13.6 us (3%)
  waiting for transfers between devices  8.74 us (2%)
  other arithmetic  5.89 us (1%)
    pallas_call x1, Pallas kernels, reduce_grads(): pl.pallas_call(functools.partial(reduce_kernel, count), out_shape=[jax.Sh...  121 us
    pallas_call x1, Pallas kernels, gather_weights(): pl.pallas_call(functools.partial(gather_kernel, count), out_shape=[jax.Sh...  119 us
    dot_general x10, matrix products, matmul(): return jnp.dot(left, right, preferred_element_type=f32)  31.4 us
    dot_general x9, matrix products, outer_sum(): lax.dot_general(left, right, (((0,), (0,)), ((), ())), preferred_element_...  24.5 us
    dot_general x8, matrix products, back_product(): lax.dot_general(left, right, (((1,), (1,)), ((), ())), preferred_element_...  21.9 us
    unnamed x90, local copies, waits for them, and re-layouts  14.3 us
    all_to_all x1, blocking collectives, body(): lax.all_to_all(outgoing.reshape(wide_count, narrow_count, capacity), 'wid...  13.6 us
    pallas_call x1, Pallas kernels, cross_backward(): pl.pallas_call(functools.partial(cross_backward_kernel, head_size), grid=...  12.5 us
  transfers between devices with their start and end apart: 5, of which 2 were waited for; matrix products, arithmetic and copies ran while one was open for 11% of the time, Pallas kernels for 50%

profile of v1, /device:TPU:0, one launch (start us, length us, event | category | flops | bytes accessed | tf_op | source)
XLA Modules:
  0.0 477.1 jit_solution(14635626447087408897)
XLA Ops:
  3.2 13.6 %all_to_all.30 = s32[8,4,12]{2,1,0:T(4,128)S(1)} all-to-all(s32[8,4,12]{2,1,0:T(4,128)S(1)} %sub.29), channel_id=1, replica_groups=mesh['wide'=8,'narrow'=4] {'wide'}, dimensions={0} | all-to-all | bytes 3072 | tf_op jit(solution)/shard_map/all_to_all | solution.py:601
  17.4 3.3 all-to-all-start.1
  32.9 8.5 %gather_fusion = bf16[384,768]{1,0:T(8,128)(2,1)S(1)} fusion(bf16[7816,768]{1,0:T(8,128)(2,1)} %param.19, s32[1024]{0:T(1024)S(1)} %pad_clamp_fusion), kind=kCustom, calls=%fused_computation | custom fusion | bytes 1181184 | tf_op jit(solution)/shard_map/gather | solution.py:613
  44.6 4.2 all-to-all-start.2
  53.9 118.6 %shard_map.238 = (bf16[4,2,2,2,24,1536]{5,4,3,2,1,0:T(8,128)(2,1)}, bf16[4,2,2,2,24,2304]{5,4,3,2,1,0:T(8,128)(2,1)}, bf16[4,2,2,2,24,768]{5,4,3,2,1,0:T(8,128)(...) custom-call(bf16[24,1536]{1,0:T(8,128)(2,1)S(1)} %copy-done.7, ...), custom_call_target="tpu_custom_call" | custom-call | tf_op jit(solution)/shard_map/pallas_call | solution.py:147
  174.5 7.1 %fusion.1.k_ref.v_ref = bf16[1536,1536]{1,0:T(8,128)(2,1)} fusion(bf16[768,1536]{1,0:T(8,128)(2,1)} %bitcast.131, bf16[1,1536,768]{2,1,0:T(8,128)(2,1)S(1)} %copy-done), kind=kOutput, calls=%fused_computation.4 | convolution fusion | flops 3626237952 | bytes 9437184 | tf_op jit(solution)/shard_map/dot_general | solution.py:32
  183.6 4.3 all-to-all-start.3
  193.9 3.7 all-to-all-done.3
  203.3 3.1 convolution_convert_fusion.2.q_ref.k_ref.v_ref
  206.4 3.8 shard_map.239
  212.6 12.0 %shard_map.240 = (bf16[192,768]{1,0:T(8,128)(2,1)S(1)}, bf16[6,1536,384]{2,1,0:T(8,128)(2,1)}) custom-call(bf16[192,768]{1,0:T(8,128)(2,1)S(1)} %convolution_convert_fusion.14.q_ref, bf16[1536,1536]{1,0:T(8,128)(2,1)S(1)} %copy-done.12, bf16[1536,1536]{1,0:T(8,128)(2,1)S(1)} %copy-done.12), custom_call_target="tpu_custom_call" | custom-call | flops 4000000000 | bytes 13000000 | tf_op jit(solution)/shard_map/pallas_call | solution.py:489
  237.4 12.5 %shard_map.241 = (bf16[192,768]{1,0:T(8,128)(2,1)S(1)}, bf16[1536,1536]{1,0:T(8,128)(2,1)S(1)}) custom-call(bf16[192,768]{1,0:T(8,128)(2,1)S(1)} %convolution_convert_fusion.14.q_ref, bf16[1536,1536]{1,0:T(8,128)(2,1)} %fusion.1.k_ref.v_ref, bf16[1536,1536]{1,0:T(8,128)(2,1)} %fusion.1.k_ref.v_ref, bf16[6,1536,384]{2,1,0:T(8,128)(2,1)} %get-tuple-element.47.prob_ref, ...), custom_call_target="tpu_custom_call" | custom-call | flops 8000000000 | bytes 18000000 | tf_op jit(solution)/shard_map/pallas_call | solution.py:512
  257.2 5.3 %shard_map.242 = (bf16[192,2304]{1,0:T(8,128)(2,1)S(1)}, f32[6,1,384]{2,1,0:T(1,128)S(1)}) custom-call(bf16[192,2304]{1,0:T(8,128)(2,1)S(1)} %convolution_convert_fusion.2.q_ref.k_ref.v_ref, bf16[192,2304]{1,0:T(8,128)(2,1)S(1)} %convolution_convert_fusion.2.q_ref.k_ref.v_ref, bf16[192,2304]{1,0:T(8,128)(2,1)S(1)} %convolution_convert_fusion.2.q_ref.k_ref.v_ref, ...), custom_call_target="tpu_custom_call" | custom-call | flops 1000000000 | bytes 4000000 | tf_op jit(solution)/shard_map/pallas_call | solution.py:459
  262.5 4.7 multiply_reduce_fusion.2
  267.2 3.0 convolution_convert_fusion.1
  275.6 5.1 %convolution_convert_fusion.3 = bf16[1536,768]{0,1:T(8,128)(2,1)} fusion(bf16[1536,1536]{1,0:T(8,128)(2,1)S(1)} %get-tuple-element.48, bf16[1,1536,768]{2,1,0:T(8,128)(2,1)S(1)} %copy-done), kind=kOutput, calls=%fused_computation.8 | convolution fusion | flops 3625058304 | bytes 9437184 | tf_op jit(solution)/shard_map/dot_general | solution.py:36
  290.2 8.7 %all-to-all-start.4 = ((bf16[8,4,12,768]{3,1,2,0:T(4,128)(2,1)}), bf16[8,4,12,768]{3,1,2,0:T(4,128)(2,1)}, u32[]{:S(2)}, u32[]{:S(2)}) async-start(bf16[8,4,12,768]{3,1,2,0:T(4,128)(2,1)} %copy.68), calls=%async_computation.4 | async-start | bytes 1179648 | tf_op jit(solution)/shard_map/all_to_all | solution.py:677
  298.9 3.8 convolution_convert_fusion.7
  303.7 121.4 %shard_map.243 = (f32[64,768]{1,0:T(8,128)}, f32[24,2048]{1,0:T(8,128)}, f32[24,2048]{1,0:T(8,128)}, f32[24,1536]{1,0:T(8,128)}, f32[24,768]{1,0:T(8,128)}, /*in...) custom-call(bf16[4,2,2,2,64,768]{5,4,3,2,1,0:T(8,128)(2,1)} %bitcast.117, ...), custom_call_target="tpu_custom_call" | custom-call | tf_op jit(solution)/shard_map/pallas_call | solution.py:299
  437.3 8.4 %fusion.3 = bf16[1,1536,768]{2,1,0:T(8,128)(2,1)} fusion(bf16[1536,1536]{1,0:T(8,128)(2,1)} %copy-done.13, bf16[768,1536]{1,0:T(8,128)(2,1)} %bitcast.132), kind=kOutput, calls=%fused_computation.13 | convolution fusion | flops 3625058304 | bytes 9437184 | tf_op jit(solution)/shard_map/dot_general | solution.py:40
  447.8 4.2 all-to-all-start.5
  452.9 3.7 fusion.14
  456.6 5.0 %all-to-all-done.5 = bf16[8,4,12,768]{3,0,2,1:T(8,128)(2,1)} async-done(((bf16[8,4,12,768]{3,0,2,1:T(8,128)(2,1)}), bf16[8,4,12,768]{3,0,2,1:T(8,128)(2,1)}, u32[]{:S(2)}, u32[]{:S(2)}) %all-to-all-start.5) | async-done | bytes 589856 | tf_op jit(solution)/shard_map/all_to_all | solution.py:676
  463.7 12.9 %fusion = f32[7816,768]{1,0:T(8,128)} fusion(bf16[384,768]{1,0:T(8,128)(2,1)} %reshape.328, s32[384]{0:T(512)S(1)} %copy-done.35), kind=kOutput, calls=%fused_computation.2 | convolution fusion | flops 4613065728 | bytes 24602112 | tf_op jit(solution)/shard_map/dot_general | solution.py:32
  (179 shorter events, 93.9 us)
Async XLA Ops:
  0.6 173.8 %copy-start = (bf16[1,1536,768]{2,1,0:T(8,128)(2,1)S(1)}, bf16[1,1536,768]{2,1,0:T(8,128)(2,1)}, u32[]{:S(2)}) copy-start(bf16[1,1536,768]{2,1,0:T(8,128)(2,1)} %param.18) | copy-start | bytes 7077892
  17.4 15.3 %all-to-all-start.1 = ((s32[8,4,12]{2,0,1:T(8,128)}), s32[8,4,12]{2,0,1:T(8,128)S(1)}, u32[]{:S(2)}, u32[]{:S(2)}) async-start(s32[8,4,12]{2,0,1:T(8,128)} %copy.61), calls=%async_computation.1 | async-start | bytes 32768 | tf_op jit(solution)/shard_map/all_to_all | solution.py:600
  32.7 8.7 %copy-start.31 = (s32[8,4,12]{2,0,1:T(8,128)}, s32[8,4,12]{2,0,1:T(8,128)S(1)}, u32[]{:S(2)}) copy-start(s32[8,4,12]{2,0,1:T(8,128)S(1)} %all-to-all-done.1) | copy-start | bytes 4612
  44.6 136.9 %all-to-all-start.2 = ((bf16[8,4,12,768]{3,1,2,0:T(4,128)(2,1)}), bf16[8,4,12,768]{3,1,2,0:T(4,128)(2,1)}, u32[]{:S(2)}, u32[]{:S(2)}) async-start(bf16[8,4,12,768]{3,1,2,0:T(4,128)(2,1)} %copy.63), calls=%async_computation.2 | async-start | bytes 1179648 | tf_op jit(solution)/shard_map/all_to_all | solution.py:615
  183.6 14.0 %all-to-all-start.3 = ((bf16[8,4,12,768]{3,0,2,1:T(8,128)(2,1)}), bf16[8,4,12,768]{3,0,2,1:T(8,128)(2,1)}, u32[]{:S(2)}, u32[]{:S(2)}) async-start(bf16[8,4,12,768]{3,0,2,1:T(8,128)(2,1)} %copy.64), calls=%async_computation.3 | async-start | bytes 1179648 | tf_op jit(solution)/shard_map/all_to_all | solution.py:614
  203.2 64.0 %copy-start.14 = (f32[192,768]{1,0:T(8,128)}, f32[192,768]{1,0:T(8,128)S(1)}, u32[]{:S(2)}) copy-start(f32[192,768]{1,0:T(8,128)S(1)} %get-tuple-element.139) | copy-start | bytes 1769476
  203.2 64.0 %copy-start.34 = (f32[192]{0:T(256)}, f32[192]{0:T(256)S(1)}, u32[]{:S(2)}) copy-start(f32[192]{0:T(256)S(1)} %fusion.50) | copy-start | bytes 2308
  206.4 4.3 copy-start.32
  212.6 12.0 %copy-start.4 = (bf16[4,2,2,2,24,768]{5,4,3,2,1,0:T(8,128)(2,1)S(1)}, bf16[4,2,2,2,24,768]{5,4,3,2,1,0:T(8,128)(2,1)}, u32[]{:S(2)}) copy-start(bf16[4,2,2,2,24,768]{5,4,3,2,1,0:T(8,128)(2,1)} %copy-done.3) | copy-start | bytes 3538948
  212.6 12.5 %copy-start.33 = (f32[768]{0:T(1024)S(1)}, f32[768]{0:T(1024)}, u32[]{:S(2)}) copy-start(f32[768]{0:T(1024)} %get-tuple-element.128) | copy-start | bytes 9220
  225.0 11.6 %copy-start.16 = (f32[192,768]{1,0:T(8,128)}, f32[192,768]{1,0:T(8,128)S(1)}, u32[]{:S(2)}) copy-start(f32[192,768]{1,0:T(8,128)S(1)} %get-tuple-element.143) | copy-start | bytes 1769476
  249.9 25.7 %copy-start.13 = (bf16[1536,1536]{1,0:T(8,128)(2,1)}, bf16[1536,1536]{1,0:T(8,128)(2,1)S(1)}, u32[]{:S(2)}) copy-start(bf16[1536,1536]{1,0:T(8,128)(2,1)S(1)} %get-tuple-element.48) | copy-start | bytes 14155780
  275.6 7.7 %copy-start.15 = (f32[192,768]{1,0:T(8,128)S(1)}, f32[192,768]{1,0:T(8,128)}, u32[]{:S(2)}) copy-start(f32[192,768]{1,0:T(8,128)} %copy-done.14) | copy-start | bytes 1769476
  285.8 13.1 %copy-start.23 = (bf16[192,2048]{1,0:T(8,128)(2,1)S(1)}, bf16[192,2048]{1,0:T(8,128)(2,1)}, u32[]{:S(2)}) copy-start(bf16[192,2048]{1,0:T(8,128)(2,1)} %get-tuple-element.135) | copy-start | bytes 2359300
  285.8 13.1 %copy-start.42 = (f32[192]{0:T(256)S(1)}, f32[192]{0:T(256)}, u32[]{:S(2)}) copy-start(f32[192]{0:T(256)} %compare_convert_fusion) | copy-start | bytes 2308
  290.2 155.5 %all-to-all-start.4 = ((bf16[8,4,12,768]{3,1,2,0:T(4,128)(2,1)}), bf16[8,4,12,768]{3,1,2,0:T(4,128)(2,1)}, u32[]{:S(2)}, u32[]{:S(2)}) async-start(bf16[8,4,12,768]{3,1,2,0:T(4,128)(2,1)} %copy.68), calls=%async_computation.4 | async-start | bytes 1179648 | tf_op jit(solution)/shard_map/all_to_all | solution.py:677
  298.9 4.2 copy-start.36
  298.9 4.2 copy-start.37
  298.9 4.2 copy-start.40
  445.7 6.3 %copy-start.29 = (f32[24,2048]{1,0:T(8,128)S(1)}, f32[24,2048]{1,0:T(8,128)}, u32[]{:S(2)}) copy-start(f32[24,2048]{1,0:T(8,128)} %get-tuple-element.58) | copy-start | bytes 589828
  445.7 6.3 %copy-start.30 = (f32[24,2048]{1,0:T(8,128)S(1)}, f32[24,2048]{1,0:T(8,128)}, u32[]{:S(2)}) copy-start(f32[24,2048]{1,0:T(8,128)} %get-tuple-element.59) | copy-start | bytes 589828
  445.7 7.2 %copy-start.17 = (f32[192,768]{1,0:T(8,128)S(1)}, f32[192,768]{1,0:T(8,128)}, u32[]{:S(2)}) copy-start(f32[192,768]{1,0:T(8,128)} %copy-done.16) | copy-start | bytes 1769476
  447.8 13.8 %all-to-all-start.5 = ((bf16[8,4,12,768]{3,0,2,1:T(8,128)(2,1)}), bf16[8,4,12,768]{3,0,2,1:T(8,128)(2,1)}, u32[]{:S(2)}, u32[]{:S(2)}) async-start(bf16[8,4,12,768]{3,0,2,1:T(8,128)(2,1)} %copy.69), calls=%async_computation.5 | async-start | bytes 1179648 | tf_op jit(solution)/shard_map/all_to_all | solution.py:676
  456.6 7.1 %copy-start.35 = (s32[384]{0:T(512)S(1)}, s32[384]{0:T(512)}, u32[]{:S(2)}) copy-start(s32[384]{0:T(512)} %eq.74) | copy-start | bytes 4612
  (25 other events, 51.9 us)
